TPU v7x, 256 devices: a whole 4x4x8 slice. The times are simulated.
256 devices in a mesh: rep: 32 (over y, x, core), head: 8 (over z).
Axes of the slice: x: 4, y: 4, z: 8, core: 2. Of those that a mesh axis runs over, the one named last changes fastest.
Arguments:
- tokens: bfloat16 [16384, 2048], P(('rep', 'head')), may hold values from -6 to 6
- parent_state: bfloat16 [128, 32, 128, 128], P('rep', 'head'), may hold values from -6 to 6
- parent_index: int32 [256], replicated, may hold values from 0 to 127, as said below
- w_qkvz: bfloat16 [2048, 12288], P(None, 'head'), may hold values from -0.125 to 0.125
- w_ba: bfloat16 [2048, 64], P(None, 'head'), may hold values from -0.125 to 0.125
- decay_rate: float32 [32], P('head'), may hold values from 0.01 to 0.12
- norm_gain: float32 [128], replicated, may hold values from 0.1 to 1.9
- w_out: bfloat16 [4096, 2048], P('head'), may hold values from -0.09375 to 0.09375
Outputs:
- mixed: bfloat16 [16384, 2048], P(('rep', 'head'))
Inputs may be any that keep to these rules, and one draw needn't show every extreme that they name: `parent_index`: children c in [r * 8, (r+1) * 8) form rep index r. For any two rep indices r and s, the children of r name at most 2 distinct parents among those of s (parents s * 4 to (s+1) * 4 - 1), and every r reaches 2 for some s.
All inputs are finite; a program needn't handle non-finite values.
Results may differ from a plain program's by a relative error of at most 0.017.
Values may be sent and summed in bfloat16 or wider, within the bound.
No kernel may reach another device: no remote copies, remote signals or barrier semaphores. Data moves between devices by JAX's collectives and lax.ppermute only.
A program may use at most 128 MiB of HBM per device.

v0:
```python
import jax
import jax.numpy as jnp
from jax import lax
from jax.sharding import PartitionSpec as P

VHEADS = 32
KHEADS = 16
DK = 128
DV = 128
SPAN = 64
CHILD_DEV = 8


def split_heads(projected, key_heads):
    row_count = projected.shape[0]
    group_ratio = VHEADS // KHEADS
    block = 2 * DK + 2 * group_ratio * DV
    main_width = key_heads * block
    main = projected[:, :main_width].reshape(row_count, key_heads, block)
    queries = main[:, :, :DK]
    keyvecs = main[:, :, DK : 2 * DK]
    values_h = main[:, :, 2 * DK : 2 * DK + group_ratio * DV].reshape(
        row_count, key_heads * group_ratio, DV
    )
    out_gate = main[:, :, 2 * DK + group_ratio * DV :].reshape(
        row_count, key_heads * group_ratio, DV
    )
    gates_raw = projected[:, main_width:].reshape(row_count, key_heads, 2 * group_ratio)
    strength_in = gates_raw[:, :, :group_ratio].reshape(row_count, key_heads * group_ratio)
    decay_in = gates_raw[:, :, group_ratio:].reshape(row_count, key_heads * group_ratio)
    return (queries, keyvecs, values_h, out_gate, strength_in, decay_in)


def delta_layer(projected, states, decay_rate, norm_gain, key_heads):
    hp = lax.Precision.HIGHEST
    children = states.shape[0]
    group_ratio = VHEADS // KHEADS
    queries, keyvecs, values_h, out_gate, strength_in, decay_in = split_heads(projected, key_heads)
    queries = (
        queries
        * lax.rsqrt(jnp.sum(queries * queries, axis=-1, keepdims=True) + 1e-06)
        * DK ** (-0.5)
    )
    keyvecs = keyvecs * lax.rsqrt(jnp.sum(keyvecs * keyvecs, axis=-1, keepdims=True) + 1e-06)
    queries = jnp.repeat(queries, group_ratio, axis=1).reshape(children, SPAN, -1, DK)
    keyvecs = jnp.repeat(keyvecs, group_ratio, axis=1).reshape(children, SPAN, -1, DK)
    values_h = values_h.reshape(children, SPAN, -1, DV)
    out_gate = out_gate.reshape(children, SPAN, -1, DV)
    strength = jax.nn.sigmoid(strength_in).reshape(children, SPAN, -1)
    log_decay = -decay_rate[None, :] * jax.nn.softplus(decay_in)
    cumulative = jnp.cumsum(log_decay.reshape(children, SPAN, -1), axis=1)
    cumul_t = jnp.transpose(cumulative, (0, 2, 1))
    strength_t = jnp.transpose(strength, (0, 2, 1))
    index_i = jnp.arange(SPAN)[:, None]
    index_j = jnp.arange(SPAN)[None, :]
    on_or_below = index_i >= index_j
    below = index_i > index_j
    decay_gap = cumul_t[..., :, None] - cumul_t[..., None, :]
    decay_mat = jnp.where(on_or_below, jnp.exp(jnp.where(on_or_below, decay_gap, 0.0)), 0.0)
    key_gram = jnp.einsum("nihd,njhd->nhij", keyvecs, keyvecs, precision=hp)
    coupling = jnp.where(below, strength_t[..., :, None] * decay_mat * key_gram, 0.0)
    identity_mat = jnp.eye(SPAN, dtype=jnp.float32)
    system = identity_mat + coupling
    keys_t = jnp.transpose(keyvecs, (0, 2, 1, 3))
    queries_t = jnp.transpose(queries, (0, 2, 1, 3))
    values_t = jnp.transpose(values_h, (0, 2, 1, 3))
    targets = jnp.concatenate(
        [(strength_t * jnp.exp(cumul_t))[..., None] * keys_t, strength_t[..., None] * values_t],
        axis=-1,
    )
    solved = lax.linalg.triangular_solve(
        system, targets, left_side=True, lower=True, unit_diagonal=True
    )
    key_part = solved[..., :DK]
    value_part = solved[..., DK:]
    corrected = value_part - jnp.einsum("nhcd,nhde->nhce", key_part, states, precision=hp)
    scores = jnp.einsum("nhid,nhjd->nhij", queries_t, keys_t, precision=hp) * decay_mat
    result = jnp.einsum(
        "nhcd,nhde->nhce", jnp.exp(cumul_t)[..., None] * queries_t, states, precision=hp
    )
    result = result + jnp.einsum("nhij,nhje->nhie", scores, corrected, precision=hp)
    result = jnp.transpose(result, (0, 2, 1, 3))
    normed = result * lax.rsqrt(jnp.mean(result * result, axis=-1, keepdims=True) + 1e-06)
    gated = normed * norm_gain * jax.nn.silu(out_gate)
    return gated.reshape(children * SPAN, -1).astype(jnp.bfloat16)


def route_states(parent_state, parent_index):
    my_rep = lax.axis_index("rep")
    my_parents = lax.dynamic_slice_in_dim(parent_index, my_rep * CHILD_DEV, CHILD_DEV)
    empty = jnp.zeros((CHILD_DEV,) + parent_state.shape[1:], jnp.float32)
    piece = lax.all_gather(parent_state, "rep", axis=0, tiled=True)
    row_count = piece.shape[0]
    selector = (my_parents[:, None] == jnp.arange(row_count, dtype=jnp.int32)[None, :]).astype(
        jnp.bfloat16
    )
    picked = jnp.dot(selector, piece.reshape(row_count, -1), preferred_element_type=jnp.float32)
    return picked.reshape(empty.shape)


def shards(tokens, parent_state, parent_index, w_qkvz, w_ba, decay_rate, norm_gain, w_out):
    key_heads = w_ba.shape[1] // 4
    child_states = None
    row_piece = lax.all_gather(tokens, "head", axis=0, tiled=True)
    projected = jnp.concatenate(
        [
            jnp.dot(row_piece, w_qkvz, preferred_element_type=jnp.float32),
            jnp.dot(row_piece, w_ba, preferred_element_type=jnp.float32),
        ],
        axis=1,
    )
    child_states = route_states(parent_state, parent_index)
    gated = delta_layer(projected, child_states, decay_rate, norm_gain, key_heads)
    return lax.psum_scatter(
        jnp.dot(gated, w_out, preferred_element_type=jnp.float32).astype(jnp.bfloat16),
        "head",
        scatter_dimension=0,
        tiled=True,
    )


def solution(mesh):
    in_specs = (
        P(("rep", "head"), None),
        P("rep", "head", None, None),
        P(),
        P(None, "head"),
        P(None, "head"),
        P("head"),
        P(),
        P("head", None),
    )
    out_specs = P(("rep", "head"), None)
    return jax.shard_map(shards, mesh=mesh, in_specs=in_specs, out_specs=out_specs, check_vma=False)
```

profile of v0, /device:TPU:2, one launch (start us, length us, event | category | flops | bytes accessed | tf_op | source)
XLA Modules:
  0.0 356.6 jit_solution(10158933316751140995)
XLA Ops:
  6.5 0.7 all-gather.3.cloned.1.call-update
  7.3 0.0 all-gather.5.cloned.1.call-start
  7.3 0.7 all-gather.5.cloned.1.call-update
  8.0 0.0 reduce-scatter.2.cloned.1.call-start
  8.1 0.7 neg.18
  8.7 0.8 dynamic_slice.3
  9.5 0.1 iota_compare_fusion.1
  9.6 43.7 %all-gather.3.cloned.1.call-done = bf16[512,2048]{1,0:T(8,128)(2,1)} async-done(((bf16[64,2048]{1,0:T(8,128)(2,1)}), bf16[512,2048]{1,0:T(8,128)(2,1)}) %all-gather.3.cloned.1.call-update) | async-done | bytes 2097168 | tf_op jit(solution)/shard_map/all_gather | solution.py:104
  53.2 2.2 fusion.45
  55.5 0.1 div.18
  55.6 0.1 reshape.75
  55.7 0.1 fusion.35
  55.8 0.2 copy.84
  56.0 6.3 %fusion.44 = f32[8,64,4]{2,0,1:T(8,128)S(1)} fusion(f32[8,64,4]{2,0,1:T(8,128)S(1)} %copy.84), kind=kOutput, calls=%fused_computation.64 | output fusion | flops 129024 | bytes 16384 | tf_op jit(solution)/shard_map/jit(cumsum)/reduce_window_sum | solution.py:51
  62.3 0.1 copy.85
  62.4 0.2 copy.94
  62.6 6.3 %fusion.46 = f32[512,1536]{0,1:T(8,128)S(1)} fusion(bf16[512,2048]{1,0:T(8,128)(2,1)} %all-gather.3.cloned.1.call-done, bf16[2048,1536]{1,0:T(8,128)(2,1)} %param.11), kind=kOutput, calls=%fused_computation.66 | convolution fusion | flops 3221225472 | bytes 11534336 | tf_op jit(solution)/shard_map/dot_general | solution.py:107
  68.9 0.1 multiply_reduce_fusion.1
  69.0 1.5 copy-done.4
  70.5 0.1 slice_multiply_fusion
  70.7 1.0 copy.91
  71.7 1.0 copy.119
  72.7 1.1 broadcast_in_dim.21
  73.8 2.8 fusion.23
  76.6 158.7 %custom-call.3 = f32[8,4,1,64,64]{3,4,2,1,0:T(8,128)} custom-call(f32[8,4,1,64,64]{4,3,2,1,0:T(8,128)} %fusion.23), custom_call_target="InvertDiagBlocksLowerTriangular" | custom-call | tf_op jit(solution)/shard_map/triangular_solve | solution.py:71
  235.3 3.1 fusion.43
  238.4 2.7 reshape.79
  241.1 3.2 copy.102
  244.2 2.7 reshape.80
  247.0 3.2 copy.107
  250.1 1.3 multiply_reduce_fusion.2
  251.5 1.2 multiply_multiply_fusion
  252.8 0.6 bitcast_multiply_fusion
  253.4 0.6 copy-done.8
  254.0 3.4 fusion.2
  257.3 0.1 broadcast_in_dim.20
  257.4 1.2 copy-done.3
  258.6 2.9 convolution_multiply_fusion.1
  261.4 24.1 %copy.112 = bf16[128,4,128,128]{0,3,2,1:T(8,128)(2,1)} copy(bf16[128,4,128,128]{3,2,1,0:T(8,128)(2,1)} %all-gather.5.cloned.1.call-done) | data formatting | bytes 33554432 | tf_op jit(solution)/shard_map/reshape | solution.py:97
  285.5 11.6 %fusion = f32[8,4,128,128]{3,0,2,1:T(8,128)} fusion(bf16[128,4,128,128]{0,3,2,1:T(8,128)(2,1)} %copy.112, s32[8]{0:T(128)S(1)} %dynamic_slice.3), kind=kOutput, calls=%fused_computation | convolution fusion | flops 134218752 | bytes 18874400 | tf_op jit(solution)/shard_map/dot_general | solution.py:97
  297.1 4.5 %fusion.16 = f32[8,4,64,128]{3,2,1,0:T(8,128)S(1)} fusion(f32[8,4,128,128]{3,0,2,1:T(8,128)} %fusion, f32[8,4,64,256]{3,2,1,0:T(8,128)} %fusion.2), kind=kOutput, calls=%fused_computation.13 | convolution fusion | flops 402915328 | bytes 5242880 | tf_op jit(solution)/shard_map/nhcd,nhde->nhce/dot_general | solution.py:76
  301.6 1.2 fusion.47
  302.8 0.4 copy-done.1
  303.2 2.4 multiply_reduce_fusion
  305.6 0.4 multiply_convert_fusion
  306.1 0.4 copy.108
  306.5 2.6 convolution_convert_fusion
  309.1 40.9 %reduce-scatter.2.cloned.1.call-done = bf16[64,2048]{1,0:T(8,128)(2,1)} async-done(((bf16[512,2048]{1,0:T(8,128)(2,1)}), bf16[64,2048]{1,0:T(8,128)(2,1)}) %reduce-scatter.2.cloned.1.call-update) | async-done | bytes 262160 | tf_op jit(solution)/shard_map/reduce_scatter | solution.py:114
  (30 shorter events, 0.2 us)
Async XLA Ops:
  6.5 300.0 %copy-start = (bf16[512,2048]{1,0:T(8,128)(2,1)S(1)}, bf16[512,2048]{1,0:T(8,128)(2,1)}, u32[]{:S(2)}) copy-start(bf16[512,2048]{1,0:T(8,128)(2,1)} %param.15) | copy-start | bytes 6291460
  6.5 46.7 %all-gather.3.cloned.1.call-start = ((), (), s32[]{:S(2)}) async-start(), calls=%async_computation.1 | async-start | bytes 2359296 | tf_op jit(solution)/shard_map/all_gather | solution.py:104
  7.3 254.2 %all-gather.5.cloned.1.call-start = ((), (), s32[]{:S(2)}) async-start(), calls=%async_computation.2 | async-start | bytes 17301504 | tf_op jit(solution)/shard_map/all_gather | solution.py:92
  8.0 342.1 %reduce-scatter.2.cloned.1.call-start = ((), (), s32[]{:S(2)}) async-start(), calls=%async_computation.3 | async-start | bytes 2359296 | tf_op jit(solution)/shard_map/reduce_scatter | solution.py:114
  68.9 1.6 copy-start.4
  73.8 178.9 %copy-start.2 = (f32[512,2,2,128]{3,0,2,1:T(8,128)}, f32[512,2,2,128]{3,0,2,1:T(8,128)S(1)}, u32[]{:S(2)}) copy-start(f32[512,2,2,128]{3,0,2,1:T(8,128)S(1)} %broadcast_in_dim.21) | copy-start | bytes 3145732
  250.1 2.6 copy-start.7
  252.8 1.2 copy-start.8
  257.3 1.2 copy-start.3
  297.1 4.5 %copy-start.5 = (f32[8,4,64,64]{3,2,1,0:T(8,128)S(1)}, f32[8,4,64,64]{3,2,1,0:T(8,128)}, u32[]{:S(2)}) copy-start(f32[8,4,64,64]{3,2,1,0:T(8,128)} %convolution_multiply_fusion.1) | copy-start | bytes 1572868
  301.6 1.6 copy-start.1
  303.2 2.4 copy-start.6
  303.2 2.4 copy-start.9
Sparse Core Ops, SparseCore 0:
  9.1 44.0 all-gather.2
  55.8 76.2 all-gather.4
  309.2 40.7 reduce-scatter.1
where the time goes:
time: 358 us; the launch traced here: 357 us
  other arithmetic  170 us (47%)
  waiting for transfers between devices  86 us (24%)
  local copies, waits for them, and re-layouts  47.7 us (13%)
  matrix products  39.8 us (11%)
  between operations  13.4 us (4%)
    another operation x2, other arithmetic, delta_layer(): lax.linalg.triangular_solve(system, targets, left_side=True, lower=True,...  159 us
    all_gather x1, waiting for transfers between devices, shards(): row_piece = lax.all_gather(tokens, 'head', axis=0, tiled=True)  43.7 us
    reduce_scatter x1, waiting for transfers between devices, shards(): lax.psum_scatter(jnp.dot(gated, w_out, preferred_element_type=jnp.float32...  40.9 us
    reshape x1, local copies, waits for them, and re-layouts, route_states(): piece.reshape(row_count, -1)  24.1 us
    dot_general x1, matrix products, route_states(): jnp.dot(selector, piece.reshape(row_count, -1), preferred_element_type=jn...  11.6 us
  transfers between devices with their start and end apart: 3, of which 2 were waited for; matrix products, arithmetic and copies ran while one was open for 58% of the time, Pallas kernels for 0%

commit v1 on v0

v1 whole, which is shorter than its diff:
```python
import functools
import jax, jax.numpy as jnp
from jax import lax
from jax.experimental import pallas as pl
from jax.experimental.pallas import tpu as pltpu
DK=128; SPAN=64
BF=jnp.bfloat16; F32=jnp.float32

def split2(a):
    hi = a.astype(BF)
    return hi, (a - hi.astype(F32)).astype(BF)

def dot_nn(a, b):
    return lax.dot_general(a, b, (((1,), (0,)), ((), ())), preferred_element_type=F32)

def dot_nt(a, b):
    return lax.dot_general(a, b, (((1,), (1,)), ((), ())), preferred_element_type=F32)

def mm3(a, b):
    ah, al = split2(a)
    bh, bl = split2(b)
    return dot_nn(jnp.concatenate([ah, al, ah], 1), jnp.concatenate([bh, bh, bl], 0))

def body(nc, ids, *refs):
    toks = refs[:nc]
    w_ref, wba_ref, dec_ref, gain_ref = refs[nc:nc+4]
    sts = refs[nc+4:2*nc+4]
    wout_ref = refs[2*nc+4]
    out_ref = refs[2*nc+5]
    rows = nc*SPAN
    x = jnp.concatenate([t[...] for t in toks], 0) if nc > 1 else toks[0][...]
    ba = dot_nn(x, wba_ref[...])
    strength = jax.nn.sigmoid(ba)
    soft = jnp.maximum(ba, 0.0) + jnp.log1p(jnp.exp(-jnp.abs(ba)))
    ld = -dec_ref[...] * soft
    ri = lax.broadcasted_iota(jnp.int32, (rows, rows), 0)
    ci = lax.broadcasted_iota(jnp.int32, (rows, rows), 1)
    tri = jnp.where((ri >= ci) & (ri // SPAN == ci // SPAN), 1.0, 0.0).astype(BF)
    l0, rest = ld.astype(BF), None
    rest = ld - l0.astype(F32)
    l1 = rest.astype(BF)
    l2 = (rest - l1.astype(F32)).astype(BF)
    cum = dot_nn(tri, l0) + dot_nn(tri, l1) + dot_nn(tri, l2)
    i2 = lax.broadcasted_iota(jnp.int32, (128, 128), 0)
    j2 = lax.broadcasted_iota(jnp.int32, (128, 128), 1)
    same = i2 // SPAN == j2 // SPAN
    incl = same & (i2 >= j2)
    strict = same & (i2 > j2)
    eye = jnp.where(i2 == j2, 1.0, 0.0).astype(F32)
    gated = []
    for g in range(2):
        blk = dot_nn(x, w_ref[:, g*768:(g+1)*768])
        q = blk[:, :128]
        k = blk[:, 128:256]
        q = q * lax.rsqrt(jnp.sum(q*q, axis=1, keepdims=True) + 1e-6) * DK**-0.5
        k = k * lax.rsqrt(jnp.sum(k*k, axis=1, keepdims=True) + 1e-6)
        tiles = []
        for n in range(nc):
            sl = slice(n*SPAN, (n+1)*SPAN)
            qh, ql = split2(q[sl]); kh, kl = split2(k[sl])
            kk = jnp.concatenate([kh, kh, kl], 1)
            qq3 = jnp.concatenate([qh, ql, qh], 1)
            kk3 = jnp.concatenate([kh, kl, kh], 1)
            gram = dot_nt(jnp.concatenate([qq3, qq3, kk3, kk3], 0), jnp.concatenate([kk, kk], 0))
            two = lambda a, c: jnp.concatenate([a[sl, c:c+1], a[sl, c+1:c+2]], 0)
            beta = two(strength, 4*g)
            gc = two(cum, 4*g+2)
            gm = jnp.broadcast_to(gc, (128, 128))
            dec = jnp.exp(jnp.where(incl, gm - gm.T, 0.0))
            amat = jnp.where(strict, beta * dec * gram[128:], 0.0)
            mmat = jnp.where(incl, dec * gram[:128], 0.0)
            sqk = jnp.concatenate([jnp.concatenate([qh, ql], 1), jnp.concatenate([kh, kl], 1)], 0)
            v2 = jnp.concatenate([blk[sl, 256:384], blk[sl, 384:512]], 0)
            z2 = jnp.concatenate([blk[sl, 512:640], blk[sl, 640:768]], 0)
            tiles.append([amat, mmat, beta, jnp.exp(gc), sqk, v2, z2, n])
        invs = [eye - jnp.where(i2 // 2 == j2 // 2, t[0], 0.0) for t in tiles]
        s = 2
        while s < SPAN:
            mask = (i2 // (2*s) == j2 // (2*s)) & ((i2 // s) % 2 == 1) & ((j2 // s) % 2 == 0)
            es = [mm3(jnp.where(mask, t[0], 0.0), d) for t, d in zip(tiles, invs)]
            invs = [d - mm3(d, e) for d, e in zip(invs, es)]
            s *= 2
        outs = []
        for t, d in zip(tiles, invs):
            amat, mmat, beta, eg, sqk, v2, z2, n = t
            st = jnp.concatenate([sts[n][0, 2*g], sts[n][0, 2*g+1]], 1)
            sp = dot_nn(sqk, jnp.concatenate([st, st], 0))
            pair = lambda a: jnp.concatenate([a[:, :128], a[:, 128:]], 0)
            r2 = beta * (v2 - eg * pair(sp[SPAN:]))
            u2 = mm3(d, r2)
            o2 = eg * pair(sp[:SPAN]) + mm3(mmat, u2)
            o2 = o2 * lax.rsqrt(jnp.mean(o2*o2, axis=1, keepdims=True) + 1e-6)
            o2 = o2 * gain_ref[...] * (z2 * jax.nn.sigmoid(z2))
            outs.append(o2.astype(BF))
        for j in range(2):
            gated.append(jnp.concatenate([o[j*SPAN:(j+1)*SPAN] for o in outs], 0) if nc > 1 else outs[0][j*SPAN:(j+1)*SPAN])
    gt = jnp.concatenate(gated, 1)
    for c in range(0, 2048, 512):
        out_ref[:, c:c+512] = dot_nn(gt, wout_ref[:, c:c+512]).astype(BF)

def delta_call(ids, tokens, w, wba, dec, gain, states, wout, nc, steps, vmem=60*2**20):
    specs = [pl.BlockSpec((SPAN, 2048), lambda i, ids, c=c: (ids[i*nc+c], 0)) for c in range(nc)]
    specs += [pl.BlockSpec((2048, 1536), lambda i, ids: (0, 0)), pl.BlockSpec((2048, 128), lambda i, ids: (0, 0)),
              pl.BlockSpec((1, 128), lambda i, ids: (0, 0)), pl.BlockSpec((1, 128), lambda i, ids: (0, 0))]
    specs += [pl.BlockSpec((1, 4, 128, 128), lambda i, ids, c=c: (ids[steps*nc+i*nc+c], 0, 0, 0)) for c in range(nc)]
    specs += [pl.BlockSpec((512, 2048), lambda i, ids: (0, 0))]
    return pl.pallas_call(
        functools.partial(body, nc),
        grid_spec=pltpu.PrefetchScalarGridSpec(num_scalar_prefetch=1, grid=(steps,), in_specs=specs,
            out_specs=pl.BlockSpec((nc*SPAN, 2048), lambda i, ids: (i, 0))),
        out_shape=jax.ShapeDtypeStruct((steps*nc*SPAN, 2048), BF),
        compiler_params=pltpu.CompilerParams(vmem_limit_bytes=vmem),
    )(ids, *([tokens]*nc), w, wba, dec, gain, *([states]*nc), wout)


from jax.sharding import PartitionSpec as P

CHILD_DEV = 8


def gate_lanes(decay_rate, w_ba):
    heads = decay_rate.shape[0]
    lanes = jnp.zeros((1, 128), F32)
    for h in range(heads):
        lanes = lanes.at[0, 4 * (h // 2) + 2 + h % 2].set(decay_rate[h])
    return lanes, jnp.pad(w_ba, ((0, 0), (0, 128 - w_ba.shape[1])))


def shards(tokens, parent_state, parent_index, w_qkvz, w_ba, decay_rate, norm_gain, w_out):
    my_rep = lax.axis_index("rep")
    mine = lax.dynamic_slice_in_dim(parent_index, my_rep * CHILD_DEV, CHILD_DEV)
    rows = lax.all_gather(tokens, "head", axis=0, tiled=True)
    states = lax.all_gather(parent_state, "rep", axis=0, tiled=True)
    lanes, wba = gate_lanes(decay_rate, w_ba)
    ids = jnp.concatenate([jnp.arange(CHILD_DEV, dtype=jnp.int32), mine])
    part = delta_call(ids, rows, w_qkvz, wba, lanes, norm_gain[None], states, w_out, 4, 2)
    return lax.psum_scatter(part, "head", scatter_dimension=0, tiled=True)


def solution(mesh):
    in_specs = (
        P(("rep", "head"), None),
        P("rep", "head", None, None),
        P(),
        P(None, "head"),
        P(None, "head"),
        P("head"),
        P(),
        P("head", None),
    )
    out_specs = P(("rep", "head"), None)
    return jax.shard_map(shards, mesh=mesh, in_specs=in_specs, out_specs=out_specs, check_vma=False)
```

time: 358 us -> 208 us (0.58)
  other arithmetic: 170 us -> 9.34 us
  waiting for transfers between devices: 86 us -> 145 us
  matrix products: 39.8 us -> 0 us
  local copies, waits for them, and re-layouts: 47.7 us -> 11.3 us
  Pallas kernels: 0 us -> 26.9 us
    another operation x3 -> x9, other arithmetic: 165 us -> 8.75 us  [the longest x2 159 us: delta_layer(): lax.linalg.triangular_solve(system, targets, left_side=True, lower=True,...]
    all_gather x2, waiting for transfers between devices: 43.7 us -> 102 us  [the longest x1 78.9 us: shards(): states = lax.all_gather(parent_state, 'rep', axis=0, tiled=True)]
    dot_general x9 -> x0, matrix products: 36.4 us -> none  [the longest x1 11.6 us: route_states(): jnp.dot(selector, piece.reshape(row_count, -1), preferred_element_type=jn...]
    pallas_call x0 -> x1, Pallas kernels: none -> 26.9 us  [delta_call(): pl.pallas_call(functools.partial(body, nc), grid_spec=pltpu.PrefetchScala...]
    reshape x3 -> x0, local copies, waits for them, and re-layouts: 24.2 us -> none  [the longest x1 24.1 us: route_states(): piece.reshape(row_count, -1)]
    another operation x5 -> x4, local copies, waits for them, and re-layouts: 11.9 us -> 2.41 us  [the longest x2 5.88 us: delta_layer(): values_h = values_h.reshape(children, SPAN, -1, DV)]
    scatter x0 -> x4, local copies, waits for them, and re-layouts: none -> 4.75 us  [gate_lanes(): lanes = lanes.at[0, 4 * (h // 2) + 2 + h % 2].set(decay_rate[h])]
    unnamed x21 -> x3, local copies, waits for them, and re-layouts: 4.7 us -> 1.04 us
  transfers between devices with their start and end apart: 3 -> 3, of which waited for: 2 -> 3; matrix products, arithmetic and copies ran while one was open for 58% -> 10% of each run, Pallas kernels for 0% -> 0%
where the time goes in v1:
time: 208 us; the launch traced here: 207 us
  waiting for transfers between devices  145 us (70%)
  Pallas kernels  26.9 us (13%)
  between operations  14.4 us (7%)
  local copies, waits for them, and re-layouts  11.3 us (5%)
  other arithmetic  9.34 us (4%)
    all_gather x1, waiting for transfers between devices, shards(): states = lax.all_gather(parent_state, 'rep', axis=0, tiled=True)  78.9 us
    reduce_scatter x1, waiting for transfers between devices, shards(): return lax.psum_scatter(part, 'head', scatter_dimension=0, tiled=True)  41.8 us
    pallas_call x1, Pallas kernels, delta_call(): pl.pallas_call(functools.partial(body, nc), grid_spec=pltpu.PrefetchScala...  26.9 us
    all_gather x1, waiting for transfers between devices, shards(): rows = lax.all_gather(tokens, 'head', axis=0, tiled=True)  23.3 us
    another operation x9, other arithmetic  8.75 us
    scatter x4, local copies, waits for them, and re-layouts, gate_lanes(): lanes = lanes.at[0, 4 * (h // 2) + 2 + h % 2].set(decay_rate[h])  4.75 us
  transfers between devices with their start and end apart: 3, of which 3 were waited for; matrix products, arithmetic and copies ran while one was open for 10% of the time, Pallas kernels for 0%

profile of v1, /device:TPU:2, one launch (start us, length us, event | category | flops | bytes accessed | tf_op | source)
XLA Modules:
  0.0 207.4 jit_solution(966714547684788187)
XLA Ops:
  6.5 0.0 all-gather.3.cloned.1.call-start
  6.5 0.7 all-gather.3.cloned.1.call-update
  7.3 0.0 all-gather.5.cloned.1.call-start
  7.3 0.7 all-gather.5.cloned.1.call-update
  8.0 0.0 reduce-scatter.2.cloned.1.call-start
  8.1 0.6 slice.93
  8.7 0.6 slice.95
  9.3 0.6 slice.97
  9.9 0.6 slice.99
  10.5 0.6 and_reduce_fusion.2
  11.1 1.5 fusion
  13.8 0.7 scatter.14
  14.6 2.6 %fusion.1 = f32[1,1]{1,0:T(1,128)} fusion(pred[1,1]{1,0:T(4,128)(4,1)} %bitcast.3, f32[1,1]{1,0:T(1,128)} %bitcast.4, f32[1,128]{1,0:T(1,128)S(1)} %scatter.14, s32[]{:T(128)} %bitcast.5), kind=kLoop, calls=%fused_computation.14 | loop fusion | flops 1 | bytes 17 | tf_op jit(solution)/shard_map/select.5
  17.1 1.3 scatter.15
  18.5 0.7 and_reduce_fusion
  19.2 2.5 %fusion.2 = f32[1,1]{1,0:T(1,128)} fusion(pred[1,1]{1,0:T(4,128)(4,1)} %bitcast.6, f32[1,1]{1,0:T(1,128)} %bitcast.7, f32[1,128]{1,0:T(1,128)S(1)} %scatter.15, s32[]{:T(128)} %bitcast.8), kind=kLoop, calls=%fused_computation.15 | loop fusion | flops 1 | bytes 17 | tf_op jit(solution)/shard_map/select.6
  21.6 1.3 scatter.16
  23.0 2.4 %fusion.3 = f32[1,1]{1,0:T(1,128)} fusion(pred[1,1]{1,0:T(4,128)(4,1)} %bitcast.9, f32[1,1]{1,0:T(1,128)} %bitcast.10, f32[1,128]{1,0:T(1,128)S(1)} %scatter.16, s32[]{:T(128)} %bitcast.11), kind=kLoop, calls=%fused_computation.16 | loop fusion | flops 1 | bytes 17 | tf_op jit(solution)/shard_map/select.7
  25.4 1.3 scatter.19.refs_6_
  26.7 0.0 copy-start
  26.7 1.0 copy.10
  27.7 0.8 dynamic_slice.3
  28.5 0.9 pad.20.refs_5_
  29.4 0.6 pad_add_fusion.ids
  30.0 23.3 %all-gather.3.cloned.1.call-done.refs_0_.refs_1_.refs_2_.refs_3_ = bf16[512,2048]{1,0:T(8,128)(2,1)} async-done(((bf16[64,2048]{1,0:T(8,128)(2,1)}), bf16[512,2048]{1,0:T(8,128)(2,1)}) %all-gather.3.cloned.1.call-update) | async-done | bytes 2097168 | tf_op jit(solution)/shard_map/all_gather | solution.py:132
  53.3 78.9 %all-gather.5.cloned.1.call-done.refs_8_.refs_9_.refs_10_.refs_11_ = bf16[128,4,128,128]{3,2,1,0:T(8,128)(2,1)} async-done(((bf16[4,4,128,128]{3,2,1,0:T(8,128)(2,1)}), bf16[128,4,128,128]{3,2,1,0:T(8,128)(2,1)}) %all-gather.5.cloned.1.call-update) | async-done | bytes 16777232 | tf_op jit(solution)/shard_map/all_gather | solution.py:133
  132.1 0.0 copy-done
  132.1 26.9 %shard_map.82 = bf16[512,2048]{1,0:T(8,128)(2,1)} custom-call(s32[16]{0:T(128)} %pad_add_fusion.ids, bf16[512,2048]{1,0:T(8,128)(2,1)} %all-gather.3.cloned.1.call-done.refs_0_.refs_1_.refs_2_.refs_3_, bf16[512,2048]{1,0:T(8,128)(2,1)} %all-gather.3.cloned.1.call-done.refs_0_.refs_1_.refs_2_.refs_3_, ...), custom_call_target="tpu_custom_call" | custom-call | tf_op jit(solution)/shard_map/pallas_call | solution.py:107
  159.1 0.0 reduce-scatter.2.cloned.1.call-update
  159.1 41.8 %reduce-scatter.2.cloned.1.call-done = bf16[64,2048]{1,0:T(8,128)(2,1)} async-done(((bf16[512,2048]{1,0:T(8,128)(2,1)}), bf16[64,2048]{1,0:T(8,128)(2,1)}) %reduce-scatter.2.cloned.1.call-update) | async-done | bytes 262160 | tf_op jit(solution)/shard_map/reduce_scatter | solution.py:137
  (6 shorter events, 0.0 us)
Async XLA Ops:
  6.5 46.8 %all-gather.3.cloned.1.call-start = ((), (), s32[]{:S(2)}) async-start(), calls=%async_computation.1 | async-start | bytes 2359296 | tf_op jit(solution)/shard_map/all_gather | solution.py:132
  7.3 124.9 %all-gather.5.cloned.1.call-start = ((), (), s32[]{:S(2)}) async-start(), calls=%async_computation.2 | async-start | bytes 17301504 | tf_op jit(solution)/shard_map/all_gather | solution.py:133
  8.0 192.9 %reduce-scatter.2.cloned.1.call-start = ((), (), s32[]{:S(2)}) async-start(), calls=%async_computation.3 | async-start | bytes 2359296 | tf_op jit(solution)/shard_map/reduce_scatter | solution.py:137
  26.7 105.5 %copy-start = (f32[1,128]{1,0:T(1,128)}, f32[1,128]{1,0:T(1,128)S(1)}, u32[]{:S(2)}) copy-start(f32[1,128]{1,0:T(1,128)S(1)} %scatter.19.refs_6_) | copy-start | bytes 1540
Sparse Core Ops, SparseCore 0:
  9.1 44.1 all-gather.2
  55.8 76.2 all-gather.4
  159.2 41.5 reduce-scatter.1
